TPU v7x, 128 devices: a whole 4x4x4 slice. The times are simulated.
128 devices in a mesh: gx: 16 (over z, y), gy: 8 (over x, core).
Axes of the slice: x: 4, y: 4, z: 4, core: 2. Of those that a mesh axis runs over, the one named last changes fastest.
Arguments:
- disp_start: float32 [3, 128, 32, 2048], P(None, 'gx', None, 'gy'), may hold values from -6 to 6
- load: float32 [3, 128, 32, 2048], P(None, 'gx', None, 'gy'), may hold values from -24 to 24
- modulus: float32 [128, 32, 2048], P('gx', None, 'gy'), may hold values from 0.5 to 2
- element_matrix: float32 [24, 24], replicated, may hold values from -0.08 to 1.2, as said below
- precond: float32 [9, 128, 32, 2048], P(None, 'gx', None, 'gy'), may hold values from -0.03 to 0.2
- approach: float32 [128], P('gx'), may hold values from 0.5 to 2.5
- contact: int32 [128, 32], P('gx', 'gy'), may hold values from 0 to 1, as said below
- owner: int32 [128, 32], P('gx', 'gy'), may hold values from 0 to 15, as said below
- slot: int32 [128, 32], P('gx', 'gy'), may hold values from 0 to 1, as said below
- influence: float32 [16, 8, 16, 2, 64, 64], P('gx', 'gy'), may hold values from -0.5 to 0.6
Outputs:
- displacement: float32 [3, 128, 32, 2048], P(None, 'gx', None, 'gy')
- pressure: float32 [128, 2048], P('gx', 'gy')
Inputs may be any that keep to these rules, and one draw needn't show every extreme that they name: `contact`: tiles outside one band of consecutive slices, wrapping around the circumference, are 0. Over the tiles of one device (8 slices by 4 tiles), the pairs (owner, slot) are all distinct, so each device hands exactly 2 tiles to each index of gx. `slot`: see owner. `element_matrix`: symmetric.
All inputs are finite; a program needn't handle non-finite values.
Results may differ from a plain program's by a relative error of at most 0.00025.
Values sent between devices are 32-bit elements; how exact they have to be, the bound alone decides.
A program may use at most 128 MiB of HBM per device.

v0:
```python
import functools

import jax
import jax.numpy as jnp
import numpy as np
from jax import lax
from jax.experimental import pallas as pl
from jax.experimental.pallas import tpu as pltpu
from jax.sharding import PartitionSpec as P

MESH = pl.DeviceIdType.MESH
F32 = jnp.float32
BF16 = jnp.bfloat16

TW = 64
PITCH = 10
penalty = 1.5
crown_depth = 0.4
crown_shape = 0.96

ROWS, HALF, COLS = 384, 192, 112


def tables():
    row = np.arange(ROWS)
    layer, c_out, i_out = row % 16, row // 16 % 2, row // 32 % 3
    b_out, a_out = row // 96 % 2, row // 192
    source = 3 * (4 * a_out + 2 * b_out + c_out) + i_out
    col = np.arange(2 * COLS)
    a_in, inner = col // COLS, col % COLS
    main = inner < 96
    node = np.where(main, inner % 16, np.where(inner < 102, 16, np.where(inner < 108, -1, -100)))
    which = np.where(main, inner // 16, (inner - 96) % 6)
    b_in, i_in = which // 3, which % 3
    dof = np.arange(24)
    pick_rows = source[:, None] == dof[None, :]
    pick_cols = np.concatenate(
        [dof[:, None] == (3 * (4 * a_in + 2 * b_in + c) + i_in)[None, :] for c in (0, 1)], axis=1
    )
    band = np.concatenate(
        [node[None, :] - layer[:, None] + c_out[:, None] == c for c in (0, 1)], axis=1
    )
    return tuple(jnp.asarray(t.astype(np.float32), BF16) for t in (pick_rows, pick_cols, band))


def split(value):
    high = value.astype(BF16)
    return high, (value - high.astype(F32)).astype(BF16)


def mm(a, b):
    return jnp.dot(a, b, preferred_element_type=F32)


def kernel(
    ngx, ngy,
    disp, load, modulus, emat, precond, approach, contact, owner, slot, influence,
    pick_rows, pick_cols, band,
    out_hbm, press_hbm,
    u1, u2, res1, res2, pre, mod, coef0, coef1, s_hi, s_lo, g_hi, g_lo,
    ext_hi, ext_lo, ext0, ext1, tot, out, press,
    em_v, rows_v, cols_v, band_v, app_v, con_v, own_v, slot_v, infl, w_hi, w_lo,
    msg_r1, msg_l1, msg_r2, msg_l2, in_r1, in_l1, in_r2, in_l2,
    send_a, recv_a, send_b, recv_b,
    local_sem, halo_send, halo_recv, a_send, a_recv, b_send, b_recv,
):
    gx, gy = lax.axis_index("gx"), lax.axis_index("gy")
    up_x, down_x = lax.rem(gx + 1, ngx), lax.rem(gx + ngx - 1, ngx)
    up_y, down_y = lax.rem(gy + 1, ngy), lax.rem(gy + ngy - 1, ngy)

    def local(i, src, dst):
        return pltpu.make_async_copy(src, dst, local_sem.at[i])

    loads = [
        local(0, disp, u1.at[:, pl.ds(1, 8)]),
        local(1, modulus, mod.at[pl.ds(1, 8)]),
        local(2, emat, em_v),
        local(3, pick_rows, rows_v),
        local(4, pick_cols, cols_v),
        local(5, band, band_v),
        local(6, load, res1),
        local(7, precond, pre),
        local(8, load, res2),
        local(9, approach, app_v),
        local(10, contact, con_v),
        local(11, owner, own_v),
        local(12, slot, slot_v),
        local(13, influence, infl),
    ]
    for c in loads:
        c.start()

    barrier = pltpu.get_barrier_semaphore()

    def greet(d, carry):
        pl.semaphore_signal(barrier, inc=1, device_id=(lax.rem(gx + d, ngx), gy), device_id_type=MESH)
        return carry

    lax.fori_loop(1, ngx, greet, 0)
    for oy in (up_y, down_y):
        for ox in (down_x, gx, up_x):
            pl.semaphore_signal(barrier, inc=1, device_id=(ox, oy), device_id_type=MESH)

    lane8 = lax.broadcasted_iota(jnp.int32, (8, 128), 1)
    lane16 = lax.broadcasted_iota(jnp.int32, (16, 128), 1)
    row16 = lax.broadcasted_iota(jnp.int32, (16, 256), 0)

    for i in (2, 3, 4, 5):
        loads[i].wait()
    for part, dst in zip(split(em_v[...]), (g_hi, g_lo)):
        wide = mm(mm(rows_v[...], part).astype(BF16), cols_v[...])
        dst[...] = (
            wide[:, : 2 * COLS] * band_v[:, : 2 * COLS].astype(F32)
            + wide[:, 2 * COLS :] * band_v[:, 2 * COLS :].astype(F32)
        ).astype(BF16)

    def pack(n, u, carry):
        left, right = carry
        for i in range(3):
            for k in range(4):
                base = (i * 4 + k) * PITCH
                hit = lane8 == base + n
                first = u[i, n, 8 * k : 8 * k + 8, 0:128]
                last = u[i, n, 8 * k : 8 * k + 8, 128:256]
                left = jnp.where(hit, pltpu.roll(first, base + n, axis=1), left)
                right = jnp.where(hit, pltpu.roll(last, base + n + 1, axis=1), right)
        return left, right

    def pack_coef(n, carry):
        for k in range(4):
            base = k * PITCH
            last = mod[n, 8 * k : 8 * k + 8, 128:256]
            carry = jnp.where(lane8 == base + n, pltpu.roll(last, base + n + 1, axis=1), carry)
        return carry

    zero8 = jnp.zeros((8, 128), F32)
    loads[0].wait()
    left, right = lax.fori_loop(1, 9, lambda n, c: pack(n, u1, c), (zero8, zero8))
    loads[1].wait()
    own_coef = lax.fori_loop(1, 9, pack_coef, zero8)
    msg_l1[0] = left
    msg_r1[0] = right
    msg_r1[1] = own_coef

    def remote(i, src, dst, to):
        return pltpu.make_async_remote_copy(
            src_ref=src, dst_ref=dst, send_sem=halo_send.at[i], recv_sem=halo_recv.at[i],
            device_id=to, device_id_type=MESH,
        )

    def columns(first, msg_l, msg_r, in_l, in_r):
        copies = []
        for d, ox in ((0, up_x), (1, gx), (2, down_x)):
            copies.append(remote(first + d, msg_r, in_r.at[d], (ox, up_y)))
            copies.append(remote(first + 3 + d, msg_l, in_l.at[d], (ox, down_y)))
        return copies

    pl.semaphore_wait(barrier, ngx - 1 + 6)
    slices1 = [
        remote(0, disp.at[:, pl.ds(7, 1)], u1.at[:, pl.ds(0, 1)], (up_x, gy)),
        remote(1, disp.at[:, pl.ds(0, 1)], u1.at[:, pl.ds(9, 1)], (down_x, gy)),
        remote(2, modulus.at[pl.ds(7, 1)], mod.at[pl.ds(0, 1)], (up_x, gy)),
    ]
    cols1 = columns(3, msg_l1, msg_r1, in_l1, in_r1)
    for c in slices1 + cols1:
        c.start()

    inside = (lax.broadcasted_iota(jnp.int32, (32, 256), 0) < 31) & (
        lax.broadcasted_iota(jnp.int32, (32, 256), 1) < 255
    )
    low_x = jnp.where(gx > 0, 1.0, 0.0).astype(F32)
    high_x = jnp.where(gx < ngx - 1, 1.0, 0.0).astype(F32)
    low_y = jnp.where(gy > 0, 1.0, 0.0).astype(F32)
    high_y = jnp.where(gy < ngy - 1, 1.0, 0.0).astype(F32)

    def set_coef(e, gain):
        value = jnp.where(inside, mod[e] * gain, 0.0)
        coef0[e] = value
        coef1[e] = pltpu.roll(value, 1, axis=0)

    def some_coef(e, carry):
        set_coef(e, jnp.where(e == 8, high_x, 1.0))
        return carry

    lax.fori_loop(1, 9, some_coef, 0)

    def operand(n, u):
        edge = [jnp.zeros((16, 256), F32), jnp.zeros((16, 256), F32)]
        for i in range(3):
            here = u[i, n]
            for b in range(2):
                value = here if b == 0 else pltpu.roll(here, 255, axis=1)
                j = b * 3 + i
                high, low = split(value)
                for g in range(2):
                    s_hi[g, n, 16 * j : 16 * j + 16] = high[16 * g : 16 * g + 16]
                    s_lo[g, n, 16 * j : 16 * j + 16] = low[16 * g : 16 * g + 16]
                edge[0] = jnp.where(row16 == j, value[16:17], edge[0])
                edge[1] = jnp.where(row16 == 6 + j, value[15:16], edge[1])
        for g in range(2):
            high, low = split(edge[g])
            s_hi[g, n, 96:112] = high
            s_lo[g, n, 96:112] = low

    def all_operands(u):
        def one(n, carry):
            operand(n, u)
            return carry

        lax.fori_loop(1, 9, one, 0)

    def product(sh, sl, start, size):
        gh, gl = g_hi[start : start + size], g_lo[start : start + size]
        return mm(gh, sh) + mm(gl, sh) + mm(gh, sl)

    def elements(e, g, sides, res):
        zs = slice(16 * g, 16 * g + 16)
        sh = s_hi[g, pl.ds(e, 2)].reshape(2 * COLS, 256)
        sl = s_lo[g, pl.ds(e, 2)].reshape(2 * COLS, 256)
        c0, c1 = coef0[e, zs], coef1[e, zs]
        r = product(sh, sl, HALF * sides[0], HALF * len(sides))
        for k, a in enumerate(sides):
            for i in range(3):
                parts = []
                for b in range(2):
                    at = ((k * 2 + b) * 3 + i) * 32
                    parts.append(r[at : at + 16] * c0 + r[at + 16 : at + 32] * c1)
                x = e - 1 + a
                res[i, x, zs] = res[i, x, zs] - (parts[0] + pltpu.roll(parts[1], 1, axis=1))

    def interior(g, res):
        def one(e, carry):
            elements(e, g, (0, 1), res)
            return carry

        lax.fori_loop(1, 8, one, 0)

    starts = [k * PITCH for k in range(12)]
    at_low = functools.reduce(jnp.logical_or, [lane8 == s for s in starts])
    at_high = functools.reduce(jnp.logical_or, [lane8 == s + 9 for s in starts])

    def merged(below, here, above):
        value = jnp.where(at_low, pltpu.roll(below, 120, axis=1), here)
        return jnp.where(at_high, pltpu.roll(above, 8, axis=1), value)

    def both(left, right, k):
        return jnp.where(
            lane8 < 64,
            pltpu.roll(left, (128 - k * PITCH) % 128, axis=1),
            pltpu.roll(right, (192 - k * PITCH) % 128, axis=1),
        )

    def ends(left, right, in_l, in_r):
        beyond_low = merged(in_r[0, 0], in_r[1, 0], in_r[2, 0])
        beyond_high = merged(in_l[0, 0], in_l[1, 0], in_l[2, 0])
        rowm = lax.broadcasted_iota(jnp.int32, (16, 128), 0)
        for b, (lo, hi) in enumerate(((beyond_low, right), (left, beyond_high))):
            for i in range(3):
                j = b * 3 + i
                here = jnp.concatenate([both(lo, hi, i * 4 + k) for k in range(4)], axis=0)
                for a in range(2):
                    value = here if a == 0 else pltpu.roll(here, 127, axis=1)
                    high, low = split(value)
                    for g in range(2):
                        at = a * COLS + 16 * j
                        ext_hi[g, at : at + 16] = high[16 * g : 16 * g + 16]
                        ext_lo[g, at : at + 16] = low[16 * g : 16 * g + 16]
                    for g, (row, source) in enumerate(((j, 16), (6 + j, 15))):
                        tot[g, a] = jnp.where(rowm == row, value[source : source + 1], 0.0 if j == 0 else tot[g, a])
        for a in range(2):
            for g in range(2):
                high, low = split(tot[g, a])
                at = a * COLS + 96
                ext_hi[g, at : at + 16] = high
                ext_lo[g, at : at + 16] = low

    def end_coef(own_coef):
        beyond = merged(in_r1[0, 1], in_r1[1, 1], in_r1[2, 1])
        gain = jnp.where(lane8 < 9, low_y, jnp.where((lane8 >= 64) & (lane8 < 73), high_y, 0.0))
        gain = jnp.where((lane8 == 0) | (lane8 == 64), gain * low_x, gain)
        gain = jnp.where((lane8 == 8) | (lane8 == 72), gain * high_x, gain)
        value = jnp.concatenate([both(beyond, own_coef, k) * gain for k in range(4)], axis=0)
        value = jnp.where(lax.broadcasted_iota(jnp.int32, (32, 128), 0) < 31, value, 0.0)
        ext0[...] = value
        ext1[...] = pltpu.roll(value, 1, axis=0)

    def end_elements(g):
        zs = slice(16 * g, 16 * g + 16)
        r = product(ext_hi[g], ext_lo[g], 0, ROWS)
        c0, c1 = ext0[zs], ext1[zs]
        for i in range(3):
            parts = []
            for a in range(2):
                at_b0, at_b1 = (a * 6 + i) * 32, (a * 6 + 3 + i) * 32
                picked = jnp.where(lane16 < 64, r[at_b1 : at_b1 + 16], r[at_b0 : at_b0 + 16])
                shifted = jnp.where(lane16 < 64, r[at_b1 + 16 : at_b1 + 32], r[at_b0 + 16 : at_b0 + 32])
                parts.append(picked * c0 + shifted * c1)
            tot[g, i] = parts[0] + pltpu.roll(parts[1], 1, axis=1)

    def update(g, x, res, u, store):
        zs = slice(16 * g, 16 * g + 16)
        resid = []
        for i in range(3):
            sides = tot[g, i]
            low = jnp.where(lane16 == 0, pltpu.roll(sides, 127 - x, axis=1), 0.0)
            high = jnp.where(lane16 == 127, pltpu.roll(sides, 62 - x, axis=1), 0.0)
            resid.append(res[i, x, zs] - jnp.concatenate([low, high], axis=1))
        for i in range(3):
            value = u[i, x + 1, zs]
            for j in range(3):
                value = value + pre[3 * i + j, x, zs] * resid[j]
            store(i, x, zs, value)

    def update_all(g, res, u, store):
        def one(x, carry):
            update(g, x, res, u, store)
            return carry

        lax.fori_loop(0, 8, one, 0)

    all_operands(u1)
    loads[6].wait()
    for g in (1, 0):
        interior(g, res1)
    for c in slices1:
        c.wait_recv()
    set_coef(0, low_x)
    operand(0, u1)
    operand(9, u1)
    for g in (1, 0):
        elements(0, g, (1,), res1)
        elements(8, g, (0,), res1)
    left, right = pack(9, u1, pack(0, u1, (msg_l1[0], msg_r1[0])))
    own_coef = pack_coef(0, msg_r1[1])
    for c in cols1:
        c.wait_recv()
    ends(left, right, in_l1, in_r1)
    end_coef(own_coef)
    for g in (1, 0):
        end_elements(g)

    def store_u2(i, x, zs, value):
        u2[i, x + 1, zs] = value

    loads[7].wait()
    for g in (1, 0):
        update_all(g, res1, u1, store_u2)
    slices2 = [
        remote(9, u2.at[:, pl.ds(8, 1)], u2.at[:, pl.ds(0, 1)], (up_x, gy)),
        remote(10, u2.at[:, pl.ds(1, 1)], u2.at[:, pl.ds(9, 1)], (down_x, gy)),
    ]
    for c in slices2:
        c.start()
    left, right = lax.fori_loop(1, 9, lambda n, c: pack(n, u2, c), (zero8, zero8))
    msg_l2[0] = left
    msg_r2[0] = right
    cols2 = columns(11, msg_l2, msg_r2, in_l2, in_r2)
    for c in cols2:
        c.start()

    all_operands(u2)
    loads[8].wait()
    interior(1, res2)
    for c in slices2:
        c.wait_recv()
    operand(0, u2)
    operand(9, u2)
    left, right = pack(9, u2, pack(0, u2, (msg_l2[0], msg_r2[0])))
    for c in cols2:
        c.wait_recv()
    ends(left, right, in_l2, in_r2)
    elements(0, 1, (1,), res2)
    elements(8, 1, (0,), res2)
    end_elements(1)

    def store_out(i, x, zs, value):
        out[i, x, zs] = value

    update_all(1, res2, u2, store_out)

    for i in (9, 10, 11, 12):
        loads[i].wait()
    lane_a = lax.broadcasted_iota(jnp.int32, (8, 8), 1)
    diag = lane_a == lax.broadcasted_iota(jnp.int32, (8, 8), 0)
    gaps = jnp.sum(jnp.where(diag, jnp.broadcast_to(app_v[...], (8, 8)), 0.0), axis=1, keepdims=True)
    y_at = (gy * 256 + lax.broadcasted_iota(jnp.int32, (1, 256), 1)).astype(F32)
    spread = (y_at + 0.5) / (256.0 * ngy) * 2.0 - 1.0
    crown = -crown_depth * jnp.log(1.0 - crown_shape * spread * spread)
    surface = jnp.concatenate([out[2, x, 31:32] for x in range(8)], axis=0)
    pen = gaps - crown - surface

    def by_tile(ref):
        return jnp.concatenate([ref[:, t : t + 1] for t in range(4)], axis=0)

    owners, slots = by_tile(own_v), by_tile(slot_v)
    lane32 = lax.broadcasted_iota(jnp.int32, (32, 128), 1)
    is_first = slots == 0

    def rolled(v):
        return pltpu.roll(v, 64, axis=1)

    halves = [pen[:, :128], pen[:, 128:]]
    tiles = jnp.concatenate([halves[0], rolled(halves[0]), halves[1], rolled(halves[1])], axis=0)
    tiles = jnp.where(lane32 < 64, tiles, 0.0)
    tiles = jnp.where(is_first, tiles, rolled(tiles))

    def exact(one_hot, value, dims):
        high, rest = split(value)
        mid, low = split(value - high.astype(F32))
        total = None
        for part in (low, mid, high):
            term = lax.dot_general(one_hot, part, (dims, ((), ())), preferred_element_type=F32)
            total = term if total is None else total + term
        return total

    to_row = jnp.where(lane32 == owners * 8, 1.0, 0.0).astype(BF16)
    send_a[...] = exact(to_row, tiles, ((0,), (0,)))

    def ring(src, dst, ssem, rsem):
        def copy(d):
            peer = lax.rem(gx + d, ngx)
            return pltpu.make_async_remote_copy(
                src_ref=src.at[pl.ds(pl.multiple_of(peer * 8, 8), 8)],
                dst_ref=dst.at[pl.ds(pl.multiple_of(gx * 8, 8), 8)],
                send_sem=ssem.at[d], recv_sem=rsem.at[d],
                device_id=(peer, gy), device_id_type=MESH,
            )

        def own():
            at = pl.ds(pl.multiple_of(gx * 8, 8), 8)
            return pltpu.make_async_copy(src.at[at], dst.at[at], ssem.at[0])

        def start(d, carry):
            copy(d).start()
            return carry

        def wait_recv(d, carry):
            copy(d).wait_recv()
            return carry

        def wait_send(d, carry):
            copy(d).wait_send()
            return carry

        def start_all():
            lax.fori_loop(1, ngx, start, 0)
            own().start()

        def arrived():
            own().wait()
            lax.fori_loop(1, ngx, wait_recv, 0)

        return start_all, arrived, lambda: lax.fori_loop(1, ngx, wait_send, 0)

    go_a, arrived_a, sent_a = ring(send_a, recv_a, a_send, a_recv)
    go_b, arrived_b, sent_b = ring(send_b, recv_b, b_send, b_recv)
    go_a()

    interior(0, res2)
    elements(0, 0, (1,), res2)
    elements(8, 0, (0,), res2)
    end_elements(0)
    update_all(0, res2, u2, store_out)
    early = local(14, out.at[:, :, pl.ds(0, 24)], out_hbm.at[:, :, pl.ds(0, 24)])
    early.start()

    loads[13].wait()

    def prepare(k, carry):
        empty = jnp.zeros((TW, TW), F32)
        rows = jnp.concatenate(
            [
                jnp.concatenate([infl[2 * k], empty], axis=1),
                jnp.concatenate([empty, infl[2 * k + 1]], axis=1),
            ],
            axis=0,
        )
        w_hi[k], w_lo[k] = split(rows)
        return carry

    lax.fori_loop(0, ngx, prepare, 0)

    arrived_a()
    got = jnp.concatenate([recv_a[8 * k : 8 * k + 1] for k in range(16)], axis=0)
    trial = penalty * jnp.maximum(got, 0.0)
    t_hi, t_lo = split(trial)
    rowk = lax.broadcasted_iota(jnp.int32, (16, 128), 0)

    def nt(a, b):
        return lax.dot_general(a, b, (((1,), (1,)), ((), ())), preferred_element_type=F32)

    change = jnp.zeros((16, 128), F32)
    for k in range(16):
        term = nt(t_hi, w_hi[k]) + nt(t_lo, w_hi[k]) + nt(t_hi, w_lo[k])
        change = jnp.where(rowk == k, term, change)
    solved = penalty * jnp.maximum(got - change, 0.0)
    for k in range(16):
        send_b[8 * k : 8 * k + 8] = jnp.broadcast_to(solved[k : k + 1], (8, 128))
    go_b()

    gain_rows = [
        jnp.concatenate([pre[3 * i + 2, x, 31:32] for x in range(8)], axis=0) for i in range(3)
    ]
    top = [jnp.concatenate([out[i, x, 31:32] for x in range(8)], axis=0) for i in range(3)]
    on = by_tile(con_v).astype(F32)
    from_row = jnp.where(lax.broadcasted_iota(jnp.int32, (32, 16), 1) == owners, 1.0, 0.0).astype(BF16)
    arrived_b()
    back = jnp.concatenate([recv_b[8 * k : 8 * k + 1] for k in range(16)], axis=0)
    home = exact(from_row, back, ((1,), (0,)))
    home = jnp.where(is_first, home, rolled(home)) * on
    first = lane8 < 64
    value = jnp.concatenate(
        [
            jnp.where(first, home[0:8], rolled(home[8:16])),
            jnp.where(first, home[16:24], rolled(home[24:32])),
        ],
        axis=1,
    )
    press[...] = value
    for i in range(3):
        fixed = top[i] - gain_rows[i] * value
        for x in range(8):
            out[i, x, 31:32] = fixed[x : x + 1]
    late = [
        local(15, out.at[:, :, pl.ds(24, 8)], out_hbm.at[:, :, pl.ds(24, 8)]),
        local(16, press, press_hbm),
    ]
    for c in late:
        c.start()
    for c in slices1 + cols1 + slices2 + cols2:
        c.wait_send()
    sent_a()
    sent_b()
    early.wait()
    for c in late:
        c.wait()


def solution(mesh):
    ngx, ngy = mesh.shape["gx"], mesh.shape["gy"]

    def per_device(
        disp_start, load, modulus, element_matrix, precond, approach, contact, owner, slot, influence
    ):
        vm = lambda shape, dtype=F32: pltpu.VMEM(shape, dtype)
        dma = lambda n: pltpu.SemaphoreType.DMA((n,))
        anywhere = pl.BlockSpec(memory_space=pl.ANY)
        return pl.pallas_call(
            functools.partial(kernel, ngx, ngy),
            out_shape=(
                jax.ShapeDtypeStruct((3, 8, 32, 256), F32),
                jax.ShapeDtypeStruct((8, 256), F32),
            ),
            in_specs=[anywhere] * 13,
            out_specs=(anywhere, anywhere),
            scratch_shapes=[
                vm((3, 10, 32, 256)), vm((3, 10, 32, 256)),
                vm((3, 8, 32, 256)), vm((3, 8, 32, 256)), vm((9, 8, 32, 256)),
                vm((9, 32, 256)), vm((9, 32, 256)), vm((9, 32, 256)),
                vm((2, 10, COLS, 256), BF16), vm((2, 10, COLS, 256), BF16),
                vm((ROWS, 2 * COLS), BF16), vm((ROWS, 2 * COLS), BF16),
                vm((2, 2 * COLS, 128), BF16), vm((2, 2 * COLS, 128), BF16),
                vm((32, 128)), vm((32, 128)), vm((2, 3, 16, 128)),
                vm((3, 8, 32, 256)), vm((8, 256)),
                vm((24, 24)), vm((ROWS, 24), BF16), vm((24, 4 * COLS), BF16), vm((ROWS, 4 * COLS), BF16),
                vm((1, 8)), vm((8, 4), jnp.int32), vm((8, 4), jnp.int32), vm((8, 4), jnp.int32),
                vm((32, TW, TW)), vm((16, 128, 128), BF16), vm((16, 128, 128), BF16),
                vm((2, 8, 128)), vm((1, 8, 128)), vm((1, 8, 128)), vm((1, 8, 128)),
                vm((3, 2, 8, 128)), vm((3, 1, 8, 128)), vm((3, 1, 8, 128)), vm((3, 1, 8, 128)),
                vm((128, 128)), vm((128, 128)), vm((128, 128)), vm((128, 128)),
                dma(17), dma(17), dma(17), dma(16), dma(16), dma(16), dma(16),
            ],
            compiler_params=pltpu.CompilerParams(
                collective_id=0, has_side_effects=True, vmem_limit_bytes=48 * 1024 * 1024
            ),
        )(
            disp_start, load, modulus, element_matrix, precond, approach.reshape(1, 8),
            contact, owner, slot, influence.reshape(32, TW, TW), *tables(),
        )

    return jax.shard_map(
        per_device,
        mesh=mesh,
        in_specs=(
            P(None, "gx", None, "gy"),
            P(None, "gx", None, "gy"),
            P("gx", None, "gy"),
            P(),
            P(None, "gx", None, "gy"),
            P("gx"),
            P("gx", "gy"),
            P("gx", "gy"),
            P("gx", "gy"),
            P("gx", "gy", None, None, None, None),
        ),
        out_specs=(P(None, "gx", None, "gy"), P("gx", "gy")),
        check_vma=False,
    )
```

profile of v0, /device:TPU:1, one launch (start us, length us, event | category | flops | bytes accessed | tf_op | source)
XLA Modules:
  0.0 50.8 jit_solution(16043523956687253226)
XLA Ops:
  0.6 0.8 %copy.15.contact = s32[8,4]{1,0:T(8,128)S(1)} copy(s32[8,4]{0,1:T(4,128)} %param.19) | data formatting | bytes 256 | tf_op args[6]
  1.4 0.8 %copy.16.owner = s32[8,4]{1,0:T(8,128)S(1)} copy(s32[8,4]{0,1:T(4,128)} %param.20) | data formatting | bytes 256 | tf_op args[7]
  2.1 0.8 %copy.17.slot = s32[8,4]{1,0:T(8,128)S(1)} copy(s32[8,4]{0,1:T(4,128)} %param.21) | data formatting | bytes 256 | tf_op args[8]
  2.9 0.0 copy-start
  2.9 1.2 %copy-done = f32[1,1,16,2,64,64]{5,4,3,2,1,0:T(8,128)S(1)} copy-done((f32[1,1,16,2,64,64]{5,4,3,2,1,0:T(8,128)S(1)}, f32[1,1,16,2,64,64]{5,4,3,2,1,0:T(8,128)}, u32[]{:S(2)}) %copy-start) | copy-done | bytes 524312
  4.1 0.0 copy-start.1
  4.1 1.1 %copy-done.1 = f32[3,8,32,256]{3,2,1,0:T(8,128)S(1)} copy-done((f32[3,8,32,256]{3,2,1,0:T(8,128)S(1)}, f32[3,8,32,256]{3,2,1,0:T(8,128)}, u32[]{:S(2)}) %copy-start.1) | copy-done | bytes 786456
  5.3 0.0 copy-start.2
  5.3 1.1 %copy-done.2 = f32[3,8,32,256]{3,2,1,0:T(8,128)S(1)} copy-done((f32[3,8,32,256]{3,2,1,0:T(8,128)S(1)}, f32[3,8,32,256]{3,2,1,0:T(8,128)}, u32[]{:S(2)}) %copy-start.2) | copy-done | bytes 786456
  6.4 0.0 copy-start.3
  6.4 1.0 %copy-done.3 = bf16[384,448]{1,0:T(8,128)(2,1)S(1)} copy-done((bf16[384,448]{1,0:T(8,128)(2,1)S(1)}, bf16[384,448]{1,0:T(8,128)(2,1)}, u32[]{:S(2)}) %copy-start.3) | copy-done | bytes 344088
  7.4 0.0 copy-start.4
  7.4 0.9 %copy-done.4 = f32[8,32,256]{2,1,0:T(8,128)S(1)} copy-done((f32[8,32,256]{2,1,0:T(8,128)S(1)}, f32[8,32,256]{2,1,0:T(8,128)}, u32[]{:S(2)}) %copy-start.4) | copy-done | bytes 262168
  8.3 0.0 copy-start.5
  8.3 0.9 %copy-done.5 = bf16[384,24]{1,0:T(8,128)(2,1)S(1)} copy-done((bf16[384,24]{1,0:T(8,128)(2,1)S(1)}, bf16[384,24]{1,0:T(8,128)(2,1)}, u32[]{:S(2)}) %copy-start.5) | copy-done | bytes 18456
  9.2 0.0 copy-start.6
  9.2 0.7 %copy-done.6 = bf16[24,448]{1,0:T(8,128)(2,1)S(1)} copy-done((bf16[24,448]{1,0:T(8,128)(2,1)S(1)}, bf16[24,448]{1,0:T(8,128)(2,1)}, u32[]{:S(2)}) %copy-start.6) | copy-done | bytes 21528
  10.0 0.0 copy-start.7
  10.0 0.7 %copy-done.7 = f32[24,24]{1,0:T(8,128)S(1)} copy-done((f32[24,24]{1,0:T(8,128)S(1)}, f32[24,24]{1,0:T(8,128)}, u32[]{:S(2)}) %copy-start.7) | copy-done | bytes 2328
  10.7 0.0 copy-start.8
  10.7 0.7 %copy-done.8 = f32[8]{0:T(128)S(1)} copy-done((f32[8]{0:T(128)S(1)}, f32[8]{0:T(128)}, u32[]{:S(2)}) %copy-start.8) | copy-done | bytes 56
  11.3 38.0 %shard_map.140 = (f32[3,8,32,256]{3,2,1,0:T(8,128)S(1)}, f32[8,256]{1,0:T(8,128)S(1)}) custom-call(f32[3,8,32,256]{3,2,1,0:T(8,128)S(1)} %copy-done.1, f32[3,8,32,256]{3,2,1,0:T(8,128)S(1)} %copy-done.2, f32[8,32,256]{2,1,0:T(8,128)S(1)} %copy-done.4, f32[24,24]{1,0:T(8,128)S(1)} %copy-done.7, f32[9,8,32,256]{3,2,1,0:T(8,128)} %precond.1, ...), custom_call_target="tpu_custom_call" | custom-call | tf_op jit(solution)/shard_map/pallas_call | solution.py:548
  49.3 0.9 %copy.20 = f32[3,8,32,256]{3,2,1,0:T(8,128)} copy(f32[3,8,32,256]{3,2,1,0:T(8,128)S(1)} %get-tuple-element.4) | data formatting | bytes 1572864
  50.2 0.6 %copy.21 = f32[8,256]{1,0:T(8,128)} copy(f32[8,256]{1,0:T(8,128)S(1)} %get-tuple-element.5) | data formatting | bytes 16384
Async XLA Ops:
  2.9 1.2 %copy-start = (f32[1,1,16,2,64,64]{5,4,3,2,1,0:T(8,128)S(1)}, f32[1,1,16,2,64,64]{5,4,3,2,1,0:T(8,128)}, u32[]{:S(2)}) copy-start(f32[1,1,16,2,64,64]{5,4,3,2,1,0:T(8,128)} %param.22) | copy-start | bytes 1572868
  4.1 1.1 %copy-start.1 = (f32[3,8,32,256]{3,2,1,0:T(8,128)S(1)}, f32[3,8,32,256]{3,2,1,0:T(8,128)}, u32[]{:S(2)}) copy-start(f32[3,8,32,256]{3,2,1,0:T(8,128)} %disp.1) | copy-start | bytes 2359300
  5.3 1.1 %copy-start.2 = (f32[3,8,32,256]{3,2,1,0:T(8,128)S(1)}, f32[3,8,32,256]{3,2,1,0:T(8,128)}, u32[]{:S(2)}) copy-start(f32[3,8,32,256]{3,2,1,0:T(8,128)} %load.1) | copy-start | bytes 2359300
  6.4 1.0 %copy-start.3 = (bf16[384,448]{1,0:T(8,128)(2,1)S(1)}, bf16[384,448]{1,0:T(8,128)(2,1)}, u32[]{:S(2)}) copy-start(bf16[384,448]{1,0:T(8,128)(2,1)} %constant.8.clone.band) | copy-start | bytes 1032196
  7.4 0.9 %copy-start.4 = (f32[8,32,256]{2,1,0:T(8,128)S(1)}, f32[8,32,256]{2,1,0:T(8,128)}, u32[]{:S(2)}) copy-start(f32[8,32,256]{2,1,0:T(8,128)} %modulus.1) | copy-start | bytes 786436
  8.3 0.9 %copy-start.5 = (bf16[384,24]{1,0:T(8,128)(2,1)S(1)}, bf16[384,24]{1,0:T(8,128)(2,1)}, u32[]{:S(2)}) copy-start(bf16[384,24]{1,0:T(8,128)(2,1)} %constant.6.clone.pick_rows) | copy-start | bytes 55300
  9.2 0.7 %copy-start.6 = (bf16[24,448]{1,0:T(8,128)(2,1)S(1)}, bf16[24,448]{1,0:T(8,128)(2,1)}, u32[]{:S(2)}) copy-start(bf16[24,448]{1,0:T(8,128)(2,1)} %constant.7.clone.pick_cols) | copy-start | bytes 64516
  10.0 0.7 %copy-start.7 = (f32[24,24]{1,0:T(8,128)S(1)}, f32[24,24]{1,0:T(8,128)}, u32[]{:S(2)}) copy-start(f32[24,24]{1,0:T(8,128)} %emat.1) | copy-start | bytes 6916
  10.7 0.7 %copy-start.8 = (f32[8]{0:T(128)S(1)}, f32[8]{0:T(128)}, u32[]{:S(2)}) copy-start(f32[8]{0:T(128)} %param.18) | copy-start | bytes 100
where the time goes:
time: 51.4 us; the launch traced here: 50.8 us
  Pallas kernels  38 us (74%)
  local copies, waits for them, and re-layouts  12.2 us (24%)
  between operations  0.65 us (1%)
    pallas_call x1, Pallas kernels, per_device(): pl.pallas_call(functools.partial(kernel, ngx, ngy), out_shape=(jax.ShapeD...  38 us
    unnamed x23, local copies, waits for them, and re-layouts  12.2 us

commit v1 on v0

--- a/solution.py
+++ b/solution.py
@@ -87,7 +87,7 @@
         local(12, slot, slot_v),
         local(13, influence, infl),
     ]
-    for c in loads:
+    for c in loads[:2]:
         c.start()
 
     barrier = pltpu.get_barrier_semaphore()
@@ -96,23 +96,31 @@
         pl.semaphore_signal(barrier, inc=1, device_id=(lax.rem(gx + d, ngx), gy), device_id_type=MESH)
         return carry
 
-    lax.fori_loop(1, ngx, greet, 0)
+    lax.fori_loop(1, ngx, greet, 0, unroll=True)
     for oy in (up_y, down_y):
         for ox in (down_x, gx, up_x):
             pl.semaphore_signal(barrier, inc=1, device_id=(ox, oy), device_id_type=MESH)
 
+    def remote(i, src, dst, to):
+        return pltpu.make_async_remote_copy(
+            src_ref=src, dst_ref=dst, send_sem=halo_send.at[i], recv_sem=halo_recv.at[i],
+            device_id=to, device_id_type=MESH,
+        )
+
+    pl.semaphore_wait(barrier, ngx - 1 + 6)
+    slices1 = [
+        remote(0, disp.at[:, pl.ds(7, 1)], u1.at[:, pl.ds(0, 1)], (up_x, gy)),
+        remote(1, disp.at[:, pl.ds(0, 1)], u1.at[:, pl.ds(9, 1)], (down_x, gy)),
+        remote(2, modulus.at[pl.ds(7, 1)], mod.at[pl.ds(0, 1)], (up_x, gy)),
+    ]
+    for c in slices1:
+        c.start()
+    for c in loads[2:]:
+        c.start()
+
     lane8 = lax.broadcasted_iota(jnp.int32, (8, 128), 1)
     lane16 = lax.broadcasted_iota(jnp.int32, (16, 128), 1)
     row16 = lax.broadcasted_iota(jnp.int32, (16, 256), 0)
-
-    for i in (2, 3, 4, 5):
-        loads[i].wait()
-    for part, dst in zip(split(em_v[...]), (g_hi, g_lo)):
-        wide = mm(mm(rows_v[...], part).astype(BF16), cols_v[...])
-        dst[...] = (
-            wide[:, : 2 * COLS] * band_v[:, : 2 * COLS].astype(F32)
-            + wide[:, 2 * COLS :] * band_v[:, 2 * COLS :].astype(F32)
-        ).astype(BF16)
 
     def pack(n, u, carry):
         left, right = carry
@@ -135,18 +143,12 @@
 
     zero8 = jnp.zeros((8, 128), F32)
     loads[0].wait()
-    left, right = lax.fori_loop(1, 9, lambda n, c: pack(n, u1, c), (zero8, zero8))
+    left, right = lax.fori_loop(1, 9, lambda n, c: pack(n, u1, c), (zero8, zero8), unroll=True)
     loads[1].wait()
-    own_coef = lax.fori_loop(1, 9, pack_coef, zero8)
+    own_coef = lax.fori_loop(1, 9, pack_coef, zero8, unroll=True)
     msg_l1[0] = left
     msg_r1[0] = right
     msg_r1[1] = own_coef
-
-    def remote(i, src, dst, to):
-        return pltpu.make_async_remote_copy(
-            src_ref=src, dst_ref=dst, send_sem=halo_send.at[i], recv_sem=halo_recv.at[i],
-            device_id=to, device_id_type=MESH,
-        )
 
     def columns(first, msg_l, msg_r, in_l, in_r):
         copies = []
@@ -155,15 +157,18 @@
             copies.append(remote(first + 3 + d, msg_l, in_l.at[d], (ox, down_y)))
         return copies
 
-    pl.semaphore_wait(barrier, ngx - 1 + 6)
-    slices1 = [
-        remote(0, disp.at[:, pl.ds(7, 1)], u1.at[:, pl.ds(0, 1)], (up_x, gy)),
-        remote(1, disp.at[:, pl.ds(0, 1)], u1.at[:, pl.ds(9, 1)], (down_x, gy)),
-        remote(2, modulus.at[pl.ds(7, 1)], mod.at[pl.ds(0, 1)], (up_x, gy)),
-    ]
     cols1 = columns(3, msg_l1, msg_r1, in_l1, in_r1)
-    for c in slices1 + cols1:
-        c.start()
+    for c in cols1:
+        c.start()
+
+    for i in (2, 3, 4, 5):
+        loads[i].wait()
+    for part, dst in zip(split(em_v[...]), (g_hi, g_lo)):
+        wide = mm(mm(rows_v[...], part).astype(BF16), cols_v[...])
+        dst[...] = (
+            wide[:, : 2 * COLS] * band_v[:, : 2 * COLS].astype(F32)
+            + wide[:, 2 * COLS :] * band_v[:, 2 * COLS :].astype(F32)
+        ).astype(BF16)
 
     inside = (lax.broadcasted_iota(jnp.int32, (32, 256), 0) < 31) & (
         lax.broadcasted_iota(jnp.int32, (32, 256), 1) < 255
@@ -182,7 +187,7 @@
         set_coef(e, jnp.where(e == 8, high_x, 1.0))
         return carry
 
-    lax.fori_loop(1, 9, some_coef, 0)
+    lax.fori_loop(1, 9, some_coef, 0, unroll=True)
 
     def operand(n, u):
         edge = [jnp.zeros((16, 256), F32), jnp.zeros((16, 256), F32)]
@@ -207,7 +212,7 @@
             operand(n, u)
             return carry
 
-        lax.fori_loop(1, 9, one, 0)
+        lax.fori_loop(1, 9, one, 0, unroll=True)
 
     def product(sh, sl, start, size):
         gh, gl = g_hi[start : start + size], g_lo[start : start + size]
@@ -233,7 +238,7 @@
             elements(e, g, (0, 1), res)
             return carry
 
-        lax.fori_loop(1, 8, one, 0)
+        lax.fori_loop(1, 8, one, 0, unroll=True)
 
     starts = [k * PITCH for k in range(12)]
     at_low = functools.reduce(jnp.logical_or, [lane8 == s for s in starts])
@@ -316,7 +321,7 @@
             update(g, x, res, u, store)
             return carry
 
-        lax.fori_loop(0, 8, one, 0)
+        lax.fori_loop(0, 8, one, 0, unroll=True)
 
     all_operands(u1)
     loads[6].wait()
@@ -351,7 +356,7 @@
     ]
     for c in slices2:
         c.start()
-    left, right = lax.fori_loop(1, 9, lambda n, c: pack(n, u2, c), (zero8, zero8))
+    left, right = lax.fori_loop(1, 9, lambda n, c: pack(n, u2, c), (zero8, zero8), unroll=True)
     msg_l2[0] = left
     msg_r2[0] = right
     cols2 = columns(11, msg_l2, msg_r2, in_l2, in_r2)
@@ -382,7 +387,11 @@
         loads[i].wait()
     lane_a = lax.broadcasted_iota(jnp.int32, (8, 8), 1)
     diag = lane_a == lax.broadcasted_iota(jnp.int32, (8, 8), 0)
-    gaps = jnp.sum(jnp.where(diag, jnp.broadcast_to(app_v[...], (8, 8)), 0.0), axis=1, keepdims=True)
+
+    def upright(row):
+        return jnp.sum(jnp.where(diag, jnp.broadcast_to(row, (8, 8)), 0.0), axis=1, keepdims=True)
+
+    gaps = upright(app_v[...])
     y_at = (gy * 256 + lax.broadcasted_iota(jnp.int32, (1, 256), 1)).astype(F32)
     spread = (y_at + 0.5) / (256.0 * ngy) * 2.0 - 1.0
     crown = -crown_depth * jnp.log(1.0 - crown_shape * spread * spread)
@@ -390,9 +399,11 @@
     pen = gaps - crown - surface
 
     def by_tile(ref):
-        return jnp.concatenate([ref[:, t : t + 1] for t in range(4)], axis=0)
-
-    owners, slots = by_tile(own_v), by_tile(slot_v)
+        value = ref[...].astype(F32)
+        return jnp.concatenate([upright(value[t : t + 1]) for t in range(4)], axis=0)
+
+    owners = by_tile(own_v).astype(jnp.int32)
+    slots = by_tile(slot_v)
     lane32 = lax.broadcasted_iota(jnp.int32, (32, 128), 1)
     is_first = slots == 0
 
@@ -443,14 +454,14 @@
             return carry
 
         def start_all():
-            lax.fori_loop(1, ngx, start, 0)
+            lax.fori_loop(1, ngx, start, 0, unroll=True)
             own().start()
 
         def arrived():
             own().wait()
-            lax.fori_loop(1, ngx, wait_recv, 0)
-
-        return start_all, arrived, lambda: lax.fori_loop(1, ngx, wait_send, 0)
+            lax.fori_loop(1, ngx, wait_recv, 0, unroll=True)
+
+        return start_all, arrived, lambda: lax.fori_loop(1, ngx, wait_send, 0, unroll=True)
 
     go_a, arrived_a, sent_a = ring(send_a, recv_a, a_send, a_recv)
     go_b, arrived_b, sent_b = ring(send_b, recv_b, b_send, b_recv)
@@ -478,7 +489,7 @@
         w_hi[k], w_lo[k] = split(rows)
         return carry
 
-    lax.fori_loop(0, ngx, prepare, 0)
+    lax.fori_loop(0, ngx, prepare, 0, unroll=True)
 
     arrived_a()
     got = jnp.concatenate([recv_a[8 * k : 8 * k + 1] for k in range(16)], axis=0)
@@ -502,7 +513,7 @@
         jnp.concatenate([pre[3 * i + 2, x, 31:32] for x in range(8)], axis=0) for i in range(3)
     ]
     top = [jnp.concatenate([out[i, x, 31:32] for x in range(8)], axis=0) for i in range(3)]
-    on = by_tile(con_v).astype(F32)
+    on = by_tile(con_v)
     from_row = jnp.where(lax.broadcasted_iota(jnp.int32, (32, 16), 1) == owners, 1.0, 0.0).astype(BF16)
     arrived_b()
     back = jnp.concatenate([recv_b[8 * k : 8 * k + 1] for k in range(16)], axis=0)
@@ -536,6 +547,20 @@
         c.wait()
 
 
+def hand_over(out, press, out_copy, press_copy, out_v, press_v, sem_in, sem_out):
+    chunks = [(r.at[i], v.at[i], c.at[i]) for r, v, c in ((out, out_v, out_copy),) for i in range(3)]
+    chunks.append((press, press_v, press_copy))
+    get = [pltpu.make_async_copy(c[0], c[1], sem_in.at[k]) for k, c in enumerate(chunks)]
+    put = [pltpu.make_async_copy(c[1], c[2], sem_out.at[k]) for k, c in enumerate(chunks)]
+    for c in get:
+        c.start()
+    for g, p in zip(get, put):
+        g.wait()
+        p.start()
+    for c in put:
+        c.wait()
+
+
 def solution(mesh):
     ngx, ngy = mesh.shape["gx"], mesh.shape["gy"]
 
@@ -544,8 +569,8 @@
     ):
         vm = lambda shape, dtype=F32: pltpu.VMEM(shape, dtype)
         dma = lambda n: pltpu.SemaphoreType.DMA((n,))
-        anywhere = pl.BlockSpec(memory_space=pl.ANY)
-        return pl.pallas_call(
+        anywhere = pl.BlockSpec(memory_space=pltpu.HBM)
+        results = pl.pallas_call(
             functools.partial(kernel, ngx, ngy),
             out_shape=(
                 jax.ShapeDtypeStruct((3, 8, 32, 256), F32),
@@ -563,7 +588,7 @@
                 vm((32, 128)), vm((32, 128)), vm((2, 3, 16, 128)),
                 vm((3, 8, 32, 256)), vm((8, 256)),
                 vm((24, 24)), vm((ROWS, 24), BF16), vm((24, 4 * COLS), BF16), vm((ROWS, 4 * COLS), BF16),
-                vm((1, 8)), vm((8, 4), jnp.int32), vm((8, 4), jnp.int32), vm((8, 4), jnp.int32),
+                vm((1, 8)), vm((4, 8), jnp.int32), vm((4, 8), jnp.int32), vm((4, 8), jnp.int32),
                 vm((32, TW, TW)), vm((16, 128, 128), BF16), vm((16, 128, 128), BF16),
                 vm((2, 8, 128)), vm((1, 8, 128)), vm((1, 8, 128)), vm((1, 8, 128)),
                 vm((3, 2, 8, 128)), vm((3, 1, 8, 128)), vm((3, 1, 8, 128)), vm((3, 1, 8, 128)),
@@ -571,12 +596,20 @@
                 dma(17), dma(17), dma(17), dma(16), dma(16), dma(16), dma(16),
             ],
             compiler_params=pltpu.CompilerParams(
-                collective_id=0, has_side_effects=True, vmem_limit_bytes=48 * 1024 * 1024
+                collective_id=0, has_side_effects=True, vmem_limit_bytes=60 * 1024 * 1024
             ),
         )(
             disp_start, load, modulus, element_matrix, precond, approach.reshape(1, 8),
-            contact, owner, slot, influence.reshape(32, TW, TW), *tables(),
+            contact.T, owner.T, slot.T, influence.reshape(32, TW, TW), *tables(),
         )
+        return pl.pallas_call(
+            hand_over,
+            out_shape=tuple(jax.ShapeDtypeStruct(r.shape, r.dtype) for r in results),
+            in_specs=[anywhere] * 2,
+            out_specs=(anywhere, anywhere),
+            scratch_shapes=[vm((3, 8, 32, 256)), vm((8, 256)), dma(4), dma(4)],
+            compiler_params=pltpu.CompilerParams(vmem_limit_bytes=60 * 1024 * 1024),
+        )(*results)
 
     return jax.shard_map(
         per_device,

time: 51.4 us -> 37.7 us (0.73)
  the two profiles are of different devices: /device:TPU:1 before, /device:TPU:0 now
where the time goes in v1:
time: 37.7 us; the launch traced here: 37.6 us
  Pallas kernels  37 us (98%)
  between operations  0.64 us (2%)
    pallas_call x1, Pallas kernels, per_device(): pl.pallas_call(functools.partial(kernel, ngx, ngy), out_shape=(jax.ShapeD...  35.1 us
    pallas_call x1, Pallas kernels, per_device(): pl.pallas_call(hand_over, out_shape=tuple((jax.ShapeDtypeStruct(r.shape,...  1.9 us

profile of v1, /device:TPU:0, one launch (start us, length us, event | category | flops | bytes accessed | tf_op | source)
XLA Modules:
  0.0 37.6 jit_solution(1054261555651199675)
XLA Ops:
  0.6 35.1 %shard_map.140 = (f32[3,8,32,256]{3,2,1,0:T(8,128)}, f32[8,256]{1,0:T(8,128)}) custom-call(f32[3,8,32,256]{3,2,1,0:T(8,128)} %disp.1, f32[3,8,32,256]{3,2,1,0:T(8,128)} %load.1, f32[8,32,256]{2,1,0:T(8,128)} %modulus.1, f32[24,24]{1,0:T(8,128)} %emat.1, f32[9,8,32,256]{3,2,1,0:T(8,128)} %precond.1, f32[1,8]{1,0:T(1,128)} %bitcast.9, s32[4,8]{1,0:T(4,128)} %bitcast.6, ...), custom_call_target="tpu_custom_call" | custom-call | tf_op jit(solution)/shard_map/pallas_call | solution.py:573
  35.7 1.9 %shard_map.141 = (f32[3,8,32,256]{3,2,1,0:T(8,128)}, f32[8,256]{1,0:T(8,128)}) custom-call(f32[3,8,32,256]{3,2,1,0:T(8,128)} %get-tuple-element.4.out, f32[8,256]{1,0:T(8,128)} %get-tuple-element.5.press), custom_call_target="tpu_custom_call" | custom-call | tf_op jit(solution)/shard_map/pallas_call | solution.py:605

commit v2 on v1

--- a/solution.py
+++ b/solution.py
@@ -61,8 +61,8 @@
     ext_hi, ext_lo, ext0, ext1, tot, out, press,
     em_v, rows_v, cols_v, band_v, app_v, con_v, own_v, slot_v, infl, w_hi, w_lo,
     msg_r1, msg_l1, msg_r2, msg_l2, in_r1, in_l1, in_r2, in_l2,
-    send_a, recv_a, send_b, recv_b,
-    local_sem, halo_send, halo_recv, a_send, a_recv, b_send, b_recv,
+    send_m, recv_m,
+    local_sem, halo_send, halo_recv, m_send, m_recv,
 ):
     gx, gy = lax.axis_index("gx"), lax.axis_index("gy")
     up_x, down_x = lax.rem(gx + 1, ngx), lax.rem(gx + ngx - 1, ngx)
@@ -160,6 +160,25 @@
     cols1 = columns(3, msg_l1, msg_r1, in_l1, in_r1)
     for c in cols1:
         c.start()
+
+
+    def matrices(d):
+        peer = lax.rem(gx + d, ngx)
+        return pltpu.make_async_remote_copy(
+            src_ref=send_m.at[peer], dst_ref=recv_m.at[gx], send_sem=m_send.at[d], recv_sem=m_recv.at[d],
+            device_id=(peer, gy), device_id_type=MESH,
+        )
+
+    def pack_matrices(k, carry):
+        send_m[k] = jnp.concatenate([infl[2 * k], infl[2 * k + 1]], axis=1)
+        return carry
+
+    loads[13].wait()
+    lax.fori_loop(0, ngx, pack_matrices, 0, unroll=True)
+    own_matrices = pltpu.make_async_copy(send_m.at[gx], recv_m.at[gx], m_send.at[0])
+    own_matrices.start()
+    for d in (1, 15, 4, 12, 2, 14, 3, 13, 5, 11, 8, 7, 9, 6, 10):
+        matrices(d).start()
 
     for i in (2, 3, 4, 5):
         loads[i].wait()
@@ -366,6 +385,20 @@
     all_operands(u2)
     loads[8].wait()
     interior(1, res2)
+    interior(0, res2)
+    own_matrices.wait()
+    for d in range(1, 16):
+        matrices(d).wait_recv()
+
+    def prepare(k, carry):
+        value = recv_m[k]
+        lane = lax.broadcasted_iota(jnp.int32, (TW, 128), 1)
+        rows = jnp.concatenate([jnp.where(lane < TW, value, 0.0), jnp.where(lane < TW, 0.0, value)], axis=0)
+        w_hi[k], w_lo[k] = split(rows)
+        return carry
+
+    lax.fori_loop(0, ngx, prepare, 0, unroll=True)
+
     for c in slices2:
         c.wait_recv()
     operand(0, u2)
@@ -424,50 +457,21 @@
             total = term if total is None else total + term
         return total
 
-    to_row = jnp.where(lane32 == owners * 8, 1.0, 0.0).astype(BF16)
-    send_a[...] = exact(to_row, tiles, ((0,), (0,)))
-
-    def ring(src, dst, ssem, rsem):
-        def copy(d):
-            peer = lax.rem(gx + d, ngx)
-            return pltpu.make_async_remote_copy(
-                src_ref=src.at[pl.ds(pl.multiple_of(peer * 8, 8), 8)],
-                dst_ref=dst.at[pl.ds(pl.multiple_of(gx * 8, 8), 8)],
-                send_sem=ssem.at[d], recv_sem=rsem.at[d],
-                device_id=(peer, gy), device_id_type=MESH,
-            )
-
-        def own():
-            at = pl.ds(pl.multiple_of(gx * 8, 8), 8)
-            return pltpu.make_async_copy(src.at[at], dst.at[at], ssem.at[0])
-
-        def start(d, carry):
-            copy(d).start()
-            return carry
-
-        def wait_recv(d, carry):
-            copy(d).wait_recv()
-            return carry
-
-        def wait_send(d, carry):
-            copy(d).wait_send()
-            return carry
-
-        def start_all():
-            lax.fori_loop(1, ngx, start, 0, unroll=True)
-            own().start()
-
-        def arrived():
-            own().wait()
-            lax.fori_loop(1, ngx, wait_recv, 0, unroll=True)
-
-        return start_all, arrived, lambda: lax.fori_loop(1, ngx, wait_send, 0, unroll=True)
-
-    go_a, arrived_a, sent_a = ring(send_a, recv_a, a_send, a_recv)
-    go_b, arrived_b, sent_b = ring(send_b, recv_b, b_send, b_recv)
-    go_a()
-
-    interior(0, res2)
+    to_owner = jnp.where(lax.broadcasted_iota(jnp.int32, (32, 16), 1) == owners, 1.0, 0.0).astype(BF16)
+    got = exact(to_owner, tiles, ((0,), (0,)))
+
+    trial = penalty * jnp.maximum(got, 0.0)
+    t_hi, t_lo = split(trial)
+    rowk = lax.broadcasted_iota(jnp.int32, (16, 128), 0)
+
+    def nt(a, b):
+        return lax.dot_general(a, b, (((1,), (1,)), ((), ())), preferred_element_type=F32)
+
+    change = jnp.zeros((16, 128), F32)
+    for k in range(16):
+        term = nt(t_hi, w_hi[k]) + nt(t_lo, w_hi[k]) + nt(t_hi, w_lo[k])
+        change = jnp.where(rowk == k, term, change)
+    solved = penalty * jnp.maximum(got - change, 0.0)
     elements(0, 0, (1,), res2)
     elements(8, 0, (0,), res2)
     end_elements(0)
@@ -475,49 +479,13 @@
     early = local(14, out.at[:, :, pl.ds(0, 24)], out_hbm.at[:, :, pl.ds(0, 24)])
     early.start()
 
-    loads[13].wait()
-
-    def prepare(k, carry):
-        empty = jnp.zeros((TW, TW), F32)
-        rows = jnp.concatenate(
-            [
-                jnp.concatenate([infl[2 * k], empty], axis=1),
-                jnp.concatenate([empty, infl[2 * k + 1]], axis=1),
-            ],
-            axis=0,
-        )
-        w_hi[k], w_lo[k] = split(rows)
-        return carry
-
-    lax.fori_loop(0, ngx, prepare, 0, unroll=True)
-
-    arrived_a()
-    got = jnp.concatenate([recv_a[8 * k : 8 * k + 1] for k in range(16)], axis=0)
-    trial = penalty * jnp.maximum(got, 0.0)
-    t_hi, t_lo = split(trial)
-    rowk = lax.broadcasted_iota(jnp.int32, (16, 128), 0)
-
-    def nt(a, b):
-        return lax.dot_general(a, b, (((1,), (1,)), ((), ())), preferred_element_type=F32)
-
-    change = jnp.zeros((16, 128), F32)
-    for k in range(16):
-        term = nt(t_hi, w_hi[k]) + nt(t_lo, w_hi[k]) + nt(t_hi, w_lo[k])
-        change = jnp.where(rowk == k, term, change)
-    solved = penalty * jnp.maximum(got - change, 0.0)
-    for k in range(16):
-        send_b[8 * k : 8 * k + 8] = jnp.broadcast_to(solved[k : k + 1], (8, 128))
-    go_b()
 
     gain_rows = [
         jnp.concatenate([pre[3 * i + 2, x, 31:32] for x in range(8)], axis=0) for i in range(3)
     ]
     top = [jnp.concatenate([out[i, x, 31:32] for x in range(8)], axis=0) for i in range(3)]
     on = by_tile(con_v)
-    from_row = jnp.where(lax.broadcasted_iota(jnp.int32, (32, 16), 1) == owners, 1.0, 0.0).astype(BF16)
-    arrived_b()
-    back = jnp.concatenate([recv_b[8 * k : 8 * k + 1] for k in range(16)], axis=0)
-    home = exact(from_row, back, ((1,), (0,)))
+    home = exact(to_owner, solved, ((1,), (0,)))
     home = jnp.where(is_first, home, rolled(home)) * on
     first = lane8 < 64
     value = jnp.concatenate(
@@ -540,8 +508,8 @@
         c.start()
     for c in slices1 + cols1 + slices2 + cols2:
         c.wait_send()
-    sent_a()
-    sent_b()
+    for d in range(1, 16):
+        matrices(d).wait_send()
     early.wait()
     for c in late:
         c.wait()
@@ -592,8 +560,8 @@
                 vm((32, TW, TW)), vm((16, 128, 128), BF16), vm((16, 128, 128), BF16),
                 vm((2, 8, 128)), vm((1, 8, 128)), vm((1, 8, 128)), vm((1, 8, 128)),
                 vm((3, 2, 8, 128)), vm((3, 1, 8, 128)), vm((3, 1, 8, 128)), vm((3, 1, 8, 128)),
-                vm((128, 128)), vm((128, 128)), vm((128, 128)), vm((128, 128)),
-                dma(17), dma(17), dma(17), dma(16), dma(16), dma(16), dma(16),
+                vm((16, TW, 128)), vm((16, TW, 128)),
+                dma(17), dma(17), dma(17), dma(16), dma(16),
             ],
             compiler_params=pltpu.CompilerParams(
                 collective_id=0, has_side_effects=True, vmem_limit_bytes=60 * 1024 * 1024

time: 37.7 us -> 31.4 us (0.83)
  the two profiles are of different devices: /device:TPU:0 before, /device:TPU:1 now
where the time goes in v2:
time: 31.4 us; the launch traced here: 31.2 us
  Pallas kernels  30.6 us (97%)
  between operations  0.64 us (2%)
    pallas_call x1, Pallas kernels, per_device(): pl.pallas_call(functools.partial(kernel, ngx, ngy), out_shape=(jax.ShapeD...  28.7 us
    pallas_call x1, Pallas kernels, per_device(): pl.pallas_call(hand_over, out_shape=tuple((jax.ShapeDtypeStruct(r.shape,...  1.9 us

profile of v2, /device:TPU:1, one launch (start us, length us, event | category | flops | bytes accessed | tf_op | source)
XLA Modules:
  0.0 31.2 jit_solution(10909425312519123697)
XLA Ops:
  0.6 28.7 %shard_map.140 = (f32[3,8,32,256]{3,2,1,0:T(8,128)}, f32[8,256]{1,0:T(8,128)}) custom-call(f32[3,8,32,256]{3,2,1,0:T(8,128)} %disp.1, f32[3,8,32,256]{3,2,1,0:T(8,128)} %load.1, f32[8,32,256]{2,1,0:T(8,128)} %modulus.1, f32[24,24]{1,0:T(8,128)} %emat.1, f32[9,8,32,256]{3,2,1,0:T(8,128)} %precond.1, f32[1,8]{1,0:T(1,128)} %bitcast.9, s32[4,8]{1,0:T(4,128)} %bitcast.6, ...), custom_call_target="tpu_custom_call" | custom-call | tf_op jit(solution)/shard_map/pallas_call | solution.py:541
  29.3 1.9 %shard_map.141 = (f32[3,8,32,256]{3,2,1,0:T(8,128)}, f32[8,256]{1,0:T(8,128)}) custom-call(f32[3,8,32,256]{3,2,1,0:T(8,128)} %get-tuple-element.4.out, f32[8,256]{1,0:T(8,128)} %get-tuple-element.5.press), custom_call_target="tpu_custom_call" | custom-call | tf_op jit(solution)/shard_map/pallas_call | solution.py:573

commit v3 on v2

--- a/solution.py
+++ b/solution.py
@@ -115,8 +115,8 @@
     ]
     for c in slices1:
         c.start()
-    for c in loads[2:]:
-        c.start()
+    for i in (2, 3, 4, 5, 13, 6, 9, 10, 11, 12, 7, 8):
+        loads[i].start()
 
     lane8 = lax.broadcasted_iota(jnp.int32, (8, 128), 1)
     lane16 = lax.broadcasted_iota(jnp.int32, (16, 128), 1)
@@ -172,13 +172,6 @@
     def pack_matrices(k, carry):
         send_m[k] = jnp.concatenate([infl[2 * k], infl[2 * k + 1]], axis=1)
         return carry
-
-    loads[13].wait()
-    lax.fori_loop(0, ngx, pack_matrices, 0, unroll=True)
-    own_matrices = pltpu.make_async_copy(send_m.at[gx], recv_m.at[gx], m_send.at[0])
-    own_matrices.start()
-    for d in (1, 15, 4, 12, 2, 14, 3, 13, 5, 11, 8, 7, 9, 6, 10):
-        matrices(d).start()
 
     for i in (2, 3, 4, 5):
         loads[i].wait()
@@ -344,8 +337,15 @@
 
     all_operands(u1)
     loads[6].wait()
-    for g in (1, 0):
-        interior(g, res1)
+    interior(1, res1)
+    interior(0, res1)
+    loads[13].wait()
+    lax.fori_loop(0, ngx, pack_matrices, 0, unroll=True)
+    own_matrices = pltpu.make_async_copy(send_m.at[gx], recv_m.at[gx], m_send.at[0])
+    own_matrices.start()
+    for d in (1, 15, 4, 12, 2, 14, 3, 13, 5, 11, 8, 7, 9, 6, 10):
+        matrices(d).start()
+
     for c in slices1:
         c.wait_recv()
     set_coef(0, low_x)
@@ -367,14 +367,18 @@
         u2[i, x + 1, zs] = value
 
     loads[7].wait()
-    for g in (1, 0):
-        update_all(g, res1, u1, store_u2)
+    for x in (0, 7):
+        for g in (1, 0):
+            update(g, x, res1, u1, store_u2)
     slices2 = [
         remote(9, u2.at[:, pl.ds(8, 1)], u2.at[:, pl.ds(0, 1)], (up_x, gy)),
         remote(10, u2.at[:, pl.ds(1, 1)], u2.at[:, pl.ds(9, 1)], (down_x, gy)),
     ]
     for c in slices2:
         c.start()
+    for x in range(1, 7):
+        for g in (1, 0):
+            update(g, x, res1, u1, store_u2)
     left, right = lax.fori_loop(1, 9, lambda n, c: pack(n, u2, c), (zero8, zero8), unroll=True)
     msg_l2[0] = left
     msg_r2[0] = right
@@ -386,19 +390,6 @@
     loads[8].wait()
     interior(1, res2)
     interior(0, res2)
-    own_matrices.wait()
-    for d in range(1, 16):
-        matrices(d).wait_recv()
-
-    def prepare(k, carry):
-        value = recv_m[k]
-        lane = lax.broadcasted_iota(jnp.int32, (TW, 128), 1)
-        rows = jnp.concatenate([jnp.where(lane < TW, value, 0.0), jnp.where(lane < TW, 0.0, value)], axis=0)
-        w_hi[k], w_lo[k] = split(rows)
-        return carry
-
-    lax.fori_loop(0, ngx, prepare, 0, unroll=True)
-
     for c in slices2:
         c.wait_recv()
     operand(0, u2)
@@ -407,14 +398,31 @@
     for c in cols2:
         c.wait_recv()
     ends(left, right, in_l2, in_r2)
-    elements(0, 1, (1,), res2)
-    elements(8, 1, (0,), res2)
-    end_elements(1)
-
     def store_out(i, x, zs, value):
         out[i, x, zs] = value
 
-    update_all(1, res2, u2, store_out)
+    early = []
+    for g in (0, 1):
+        elements(0, g, (1,), res2)
+        elements(8, g, (0,), res2)
+        end_elements(g)
+        update_all(g, res2, u2, store_out)
+        zs = pl.ds(16 * g, 16 - 8 * g)
+        early.append(local(14 + g, out.at[:, :, zs], out_hbm.at[:, :, zs]))
+        early[g].start()
+
+    own_matrices.wait()
+    for d in range(1, 16):
+        matrices(d).wait_recv()
+
+    def prepare(k, carry):
+        value = recv_m[k]
+        lane = lax.broadcasted_iota(jnp.int32, (TW, 128), 1)
+        rows = jnp.concatenate([jnp.where(lane < TW, value, 0.0), jnp.where(lane < TW, 0.0, value)], axis=0)
+        w_hi[k], w_lo[k] = split(rows)
+        return carry
+
+    lax.fori_loop(0, ngx, prepare, 0, unroll=True)
 
     for i in (9, 10, 11, 12):
         loads[i].wait()
@@ -472,14 +480,6 @@
         term = nt(t_hi, w_hi[k]) + nt(t_lo, w_hi[k]) + nt(t_hi, w_lo[k])
         change = jnp.where(rowk == k, term, change)
     solved = penalty * jnp.maximum(got - change, 0.0)
-    elements(0, 0, (1,), res2)
-    elements(8, 0, (0,), res2)
-    end_elements(0)
-    update_all(0, res2, u2, store_out)
-    early = local(14, out.at[:, :, pl.ds(0, 24)], out_hbm.at[:, :, pl.ds(0, 24)])
-    early.start()
-
-
     gain_rows = [
         jnp.concatenate([pre[3 * i + 2, x, 31:32] for x in range(8)], axis=0) for i in range(3)
     ]
@@ -501,8 +501,8 @@
         for x in range(8):
             out[i, x, 31:32] = fixed[x : x + 1]
     late = [
-        local(15, out.at[:, :, pl.ds(24, 8)], out_hbm.at[:, :, pl.ds(24, 8)]),
-        local(16, press, press_hbm),
+        local(16, out.at[:, :, pl.ds(24, 8)], out_hbm.at[:, :, pl.ds(24, 8)]),
+        local(17, press, press_hbm),
     ]
     for c in late:
         c.start()
@@ -510,8 +510,7 @@
         c.wait_send()
     for d in range(1, 16):
         matrices(d).wait_send()
-    early.wait()
-    for c in late:
+    for c in early + late:
         c.wait()
 
 
@@ -561,7 +560,7 @@
                 vm((2, 8, 128)), vm((1, 8, 128)), vm((1, 8, 128)), vm((1, 8, 128)),
                 vm((3, 2, 8, 128)), vm((3, 1, 8, 128)), vm((3, 1, 8, 128)), vm((3, 1, 8, 128)),
                 vm((16, TW, 128)), vm((16, TW, 128)),
-                dma(17), dma(17), dma(17), dma(16), dma(16),
+                dma(18), dma(17), dma(17), dma(16), dma(16),
             ],
             compiler_params=pltpu.CompilerParams(
                 collective_id=0, has_side_effects=True, vmem_limit_bytes=60 * 1024 * 1024

time: 31.4 us -> 30.3 us (0.965)
  Pallas kernels: 30.6 us -> 29.5 us
    pallas_call x1, Pallas kernels: 28.7 us -> 27.6 us  [per_device(): pl.pallas_call(functools.partial(kernel, ngx, ngy), out_shape=(jax.ShapeD...]
where the time goes in v3:
time: 30.3 us; the launch traced here: 30.1 us
  Pallas kernels  29.5 us (97%)
  between operations  0.64 us (2%)
    pallas_call x1, Pallas kernels, per_device(): pl.pallas_call(functools.partial(kernel, ngx, ngy), out_shape=(jax.ShapeD...  27.6 us
    pallas_call x1, Pallas kernels, per_device(): pl.pallas_call(hand_over, out_shape=tuple((jax.ShapeDtypeStruct(r.shape,...  1.9 us

profile of v3, /device:TPU:1, one launch (start us, length us, event | category | flops | bytes accessed | tf_op | source)
XLA Modules:
  0.0 30.1 jit_solution(1680407200004683355)
XLA Ops:
  0.6 27.6 %shard_map.140 = (f32[3,8,32,256]{3,2,1,0:T(8,128)}, f32[8,256]{1,0:T(8,128)}) custom-call(f32[3,8,32,256]{3,2,1,0:T(8,128)} %disp.1, f32[3,8,32,256]{3,2,1,0:T(8,128)} %load.1, f32[8,32,256]{2,1,0:T(8,128)} %modulus.1, f32[24,24]{1,0:T(8,128)} %emat.1, f32[9,8,32,256]{3,2,1,0:T(8,128)} %precond.1, f32[1,8]{1,0:T(1,128)} %bitcast.9, s32[4,8]{1,0:T(4,128)} %bitcast.6, ...), custom_call_target="tpu_custom_call" | custom-call | tf_op jit(solution)/shard_map/pallas_call | solution.py:540
  28.2 1.9 %shard_map.141 = (f32[3,8,32,256]{3,2,1,0:T(8,128)}, f32[8,256]{1,0:T(8,128)}) custom-call(f32[3,8,32,256]{3,2,1,0:T(8,128)} %get-tuple-element.4.out, f32[8,256]{1,0:T(8,128)} %get-tuple-element.5.press), custom_call_target="tpu_custom_call" | custom-call | tf_op jit(solution)/shard_map/pallas_call | solution.py:572

commit v4 on v3

--- a/solution.py
+++ b/solution.py
@@ -343,7 +343,7 @@
     lax.fori_loop(0, ngx, pack_matrices, 0, unroll=True)
     own_matrices = pltpu.make_async_copy(send_m.at[gx], recv_m.at[gx], m_send.at[0])
     own_matrices.start()
-    for d in (1, 15, 4, 12, 2, 14, 3, 13, 5, 11, 8, 7, 9, 6, 10):
+    for d in (10, 6, 9, 11, 7, 5, 14, 2, 8, 13, 3, 15, 1, 12, 4):
         matrices(d).start()
 
     for c in slices1:

time: 30.3 us -> 30 us (0.990)
  no operation moved by 1% of the time
where the time goes in v4:
time: 30 us; the launch traced here: 29.9 us
  Pallas kernels  29.3 us (98%)
  between operations  0.64 us (2%)
    pallas_call x1, Pallas kernels, per_device(): pl.pallas_call(functools.partial(kernel, ngx, ngy), out_shape=(jax.ShapeD...  27.4 us
    pallas_call x1, Pallas kernels, per_device(): pl.pallas_call(hand_over, out_shape=tuple((jax.ShapeDtypeStruct(r.shape,...  1.9 us

profile of v4, /device:TPU:1, one launch (start us, length us, event | category | flops | bytes accessed | tf_op | source)
XLA Modules:
  0.0 29.9 jit_solution(1318953768213135522)
XLA Ops:
  0.6 27.4 %shard_map.140 = (f32[3,8,32,256]{3,2,1,0:T(8,128)}, f32[8,256]{1,0:T(8,128)}) custom-call(f32[3,8,32,256]{3,2,1,0:T(8,128)} %disp.1, f32[3,8,32,256]{3,2,1,0:T(8,128)} %load.1, f32[8,32,256]{2,1,0:T(8,128)} %modulus.1, f32[24,24]{1,0:T(8,128)} %emat.1, f32[9,8,32,256]{3,2,1,0:T(8,128)} %precond.1, f32[1,8]{1,0:T(1,128)} %bitcast.9, s32[4,8]{1,0:T(4,128)} %bitcast.6, ...), custom_call_target="tpu_custom_call" | custom-call | tf_op jit(solution)/shard_map/pallas_call | solution.py:540
  28.0 1.9 %shard_map.141 = (f32[3,8,32,256]{3,2,1,0:T(8,128)}, f32[8,256]{1,0:T(8,128)}) custom-call(f32[3,8,32,256]{3,2,1,0:T(8,128)} %get-tuple-element.4.out, f32[8,256]{1,0:T(8,128)} %get-tuple-element.5.press), custom_call_target="tpu_custom_call" | custom-call | tf_op jit(solution)/shard_map/pallas_call | solution.py:572
